TPU v7x, 512 devices: a whole 4x8x8 slice. The times are simulated.
512 devices in a mesh: ctx: 64 (over y_lo, z, x), tp: 8 (over y_hi, core).
Axes of the slice: x: 4, y: 8 (y_hi: 4, y_lo: 2; y = y_hi * 2 + y_lo), z: 8, core: 2. Of those that a mesh axis runs over, the one named last changes fastest.
Arguments:
- queries: bfloat16 [16384, 8192], P('ctx', 'tp'), may hold values from -128 to 128
- cotangent: bfloat16 [16384, 8192], P('ctx', 'tp'), may hold values from -96 to 96
- image_keys: bfloat16 [64, 64, 1024], P('ctx', None, 'tp'), may hold values from -8 to 8
- image_values: bfloat16 [64, 64, 1024], P('ctx', None, 'tp'), may hold values from -6 to 6
- attn_gate: float32 [1], replicated, may hold values from 0.4 to 1.5
- block_mask: int32 [128, 64], P('ctx'), may hold values from 0 to 1, as said below
- image_owner: int32 [64], replicated, may hold values from 0 to 63, each once
Outputs:
- query_grad: bfloat16 [16384, 8192], P('ctx', 'tp')
- key_grad: bfloat16 [64, 64, 1024], P('ctx', None, 'tp')
- value_grad: bfloat16 [64, 64, 1024], P('ctx', None, 'tp')
- gate_grad: float32 [1], replicated
Inputs may be any that keep to these rules, and one draw needn't show every extreme that they name: `block_mask`: every text block reads at least one image; the 2 blocks of one index of ctx together read exactly 32 distinct images.
All inputs are finite; a program needn't handle non-finite values.
Results may differ from a plain program's by a relative error of at most 0.02.
Values may be sent and summed in bfloat16 or wider, within the bound.
A program may use at most 64 MiB of HBM per device.

v0:
```python
import math
import jax
import jax.numpy as jnp
from jax import lax
from jax.sharding import PartitionSpec as P

HD = 128
BLK = 128


def per_device(queries, cotangent, image_keys, image_values, attn_gate, block_mask, image_owner):
    tok_dev = queries.shape[0]
    local_kv = image_keys.shape[2] // HD
    local_heads = queries.shape[1] // HD
    groups = local_heads // local_kv
    img_tok = image_keys.shape[1]
    inv_root = 1.0 / math.sqrt(HD)
    read_most = lax.axis_size("ctx") // 2
    gathered_keys, gathered_values = (
        lax.all_gather(image_keys, "ctx", axis=0, tiled=True),
        lax.all_gather(image_values, "ctx", axis=0, tiled=True),
    )
    n_images = gathered_keys.shape[0]
    read_any = jnp.max(block_mask, axis=0)
    ranking = read_any * (2 * n_images) + (n_images - 1 - jnp.arange(n_images, dtype=jnp.int32))
    top_vals, image_ids = lax.top_k(ranking, read_most)
    is_read = read_any[image_ids] > 0
    slot_ids = image_owner[image_ids]
    block_keep = (block_mask[:, image_ids] > 0) & is_read[None, :]
    keep_mask = jnp.repeat(jnp.repeat(block_keep, BLK, axis=0), img_tok, axis=1)
    key_rows = jnp.take(gathered_keys, slot_ids, axis=0).reshape(read_most * img_tok, local_kv, HD)
    value_rows = jnp.take(gathered_values, slot_ids, axis=0).reshape(
        read_most * img_tok, local_kv, HD
    )
    query_heads = queries.reshape(tok_dev, local_kv, groups, HD).transpose(2, 0, 1, 3)
    cot_heads = cotangent.reshape(tok_dev, local_kv, groups, HD).transpose(2, 0, 1, 3)
    gate_value = jnp.tanh(attn_gate[0])

    def head_step(state_in, head_inputs):
        key_acc, value_acc, gate_acc = state_in
        query_one, cot_one = head_inputs
        scores = (
            jnp.einsum("tkd,skd->kts", query_one, key_rows, preferred_element_type=jnp.float32)
            * inv_root
        )
        scores = jnp.where(keep_mask, scores, -1e30)
        row_max = jnp.max(scores, axis=-1, keepdims=True)
        exp_terms = jnp.where(keep_mask, jnp.exp(scores - row_max), 0.0)
        prob_full = exp_terms / jnp.sum(exp_terms, axis=-1, keepdims=True)
        prob_half = prob_full.astype(jnp.bfloat16)
        attended = jnp.einsum(
            "kts,skd->tkd", prob_half, value_rows, preferred_element_type=jnp.float32
        )
        cot_f = cot_one.astype(jnp.float32)
        gate_part = jnp.sum(cot_f * attended)
        attn_grad = (gate_value * cot_f).astype(jnp.bfloat16)
        prob_grad = jnp.einsum(
            "tkd,skd->kts", attn_grad, value_rows, preferred_element_type=jnp.float32
        )
        row_delta = jnp.sum(attn_grad.astype(jnp.float32) * attended, axis=-1).T
        score_grad = (prob_full * (prob_grad - row_delta[:, :, None]) * inv_root).astype(
            jnp.bfloat16
        )
        query_grad = jnp.einsum(
            "kts,skd->tkd", score_grad, key_rows, preferred_element_type=jnp.float32
        ).astype(jnp.bfloat16)
        key_acc = key_acc + jnp.einsum(
            "kts,tkd->skd", score_grad, query_one, preferred_element_type=jnp.float32
        )
        value_acc = value_acc + jnp.einsum(
            "kts,tkd->skd", prob_half, attn_grad, preferred_element_type=jnp.float32
        )
        return ((key_acc, value_acc, gate_acc + gate_part), query_grad)

    zero_grads = jnp.zeros((read_most * img_tok, local_kv, HD), jnp.float32)
    init_state = (zero_grads, zero_grads, jnp.zeros((), jnp.float32))
    (key_acc, value_acc, gate_acc), head_grads = lax.scan(
        head_step, init_state, (query_heads, cot_heads)
    )
    query_grad = head_grads.transpose(1, 2, 0, 3).reshape(tok_dev, local_heads * HD)
    stacked = jnp.concatenate(
        [
            key_acc.reshape(read_most, img_tok, local_kv * HD),
            value_acc.reshape(read_most, img_tok, local_kv * HD),
        ],
        axis=-1,
    )
    stacked = jnp.where(is_read[:, None, None], stacked, 0.0)
    buffer = (
        jnp.zeros((n_images, img_tok, 2 * local_kv * HD), jnp.float32).at[slot_ids].add(stacked)
    )
    received = lax.all_to_all(buffer, "ctx", split_axis=0, concat_axis=0, tiled=True)
    summed = jnp.sum(received, axis=0, keepdims=True)
    key_grad = summed[:, :, : local_kv * HD].astype(jnp.bfloat16)
    value_grad = summed[:, :, local_kv * HD :].astype(jnp.bfloat16)
    gate_total = lax.psum(gate_acc, ("ctx", "tp"))
    term_count = tok_dev * lax.axis_size("ctx") * local_heads * lax.axis_size("tp") * HD
    gate_grad = ((1.0 - gate_value * gate_value) * gate_total / math.sqrt(term_count)).reshape(1)
    return (query_grad, key_grad, value_grad, gate_grad)


def solution(mesh):
    in_specs = (
        P("ctx", "tp"),
        P("ctx", "tp"),
        P("ctx", None, "tp"),
        P("ctx", None, "tp"),
        P(),
        P("ctx", None),
        P(),
    )
    out_specs = (P("ctx", "tp"), P("ctx", None, "tp"), P("ctx", None, "tp"), P())
    return jax.shard_map(
        per_device, mesh=mesh, in_specs=in_specs, out_specs=out_specs, check_vma=False
    )
```

profile of v0, /device:TPU:1, one launch (start us, length us, event | category | flops | bytes accessed | tf_op | source)
XLA Modules:
  0.0 885.6 jit_solution(12151461978923027463)
XLA Ops:
  10.9 2.0 top_k.11
  15.1 1.2 copy.35
  17.4 253.3 %all-gather.5.cloned.1.call-done = bf16[64,64,128]{2,1,0:T(8,128)(2,1)} async-done(((bf16[1,64,128]{2,1,0:T(8,128)(2,1)}), bf16[64,64,128]{2,1,0:T(8,128)(2,1)}) %all-gather.5.cloned.1.call-update) | async-done | bytes 1048592 | tf_op jit(solution)/shard_map/all_gather | solution.py:21
  270.7 1.9 gather_fusion.4
  272.6 297.7 %all-gather.3.cloned.1.call-done = bf16[64,64,128]{2,1,0:T(8,128)(2,1)} async-done(((bf16[1,64,128]{2,1,0:T(8,128)(2,1)}), bf16[64,64,128]{2,1,0:T(8,128)(2,1)}) %all-gather.3.cloned.1.call-update) | async-done | bytes 1048592 | tf_op jit(solution)/shard_map/all_gather | solution.py:20
  570.4 1.9 gather_fusion.3
  572.4 92.9 %while.17 = (s32[]{:T(128)}, f32[2048,1,128]{0,2,1:T(8,128)}, f32[2048,1,128]{0,2,1:T(8,128)}, f32[]{:T(128)}, bf16[8,256,1,128]{3,1,2,0:T(8,128)(2,1)}, /*index...) while((s32[]{:T(128)}, f32[2048,1,128]{0,2,1:T(8,128)}, ...), condition=%wide.region_7.9_spmd.clone, body=%wide.region_2.8_spmd.clone.sunk | while | flops 814710016 | bytes 48644448 | solution.py:77
  575.2 1.9 fusion.68
  577.8 1.4 fusion.69
  579.3 1.4 fusion.71
  580.7 1.1 fusion.72
  581.8 1.3 fusion.70
  586.8 1.9 fusion.68
  589.4 1.4 fusion.69
  590.9 1.4 fusion.71
  593.4 1.3 fusion.70
  598.4 1.9 fusion.68
  601.0 1.4 fusion.69
  602.5 1.4 fusion.71
  605.0 1.3 fusion.70
  610.1 1.9 fusion.68
  612.7 1.4 fusion.69
  614.1 1.4 fusion.71
  616.6 1.3 fusion.70
  621.7 1.9 fusion.68
  624.3 1.4 fusion.69
  625.7 1.4 fusion.71
  628.2 1.3 fusion.70
  633.3 1.9 fusion.68
  635.9 1.4 fusion.69
  637.3 1.4 fusion.71
  639.8 1.3 fusion.70
  644.9 1.9 fusion.68
  647.5 1.4 fusion.69
  649.0 1.4 fusion.71
  651.4 1.3 fusion.70
  656.5 1.9 fusion.68
  659.1 1.4 fusion.69
  660.6 1.4 fusion.71
  663.1 1.3 fusion.70
  665.3 1.6 copy.40
  667.0 1.3 copy.41
  668.3 1.4 maximum_select_fusion
  669.8 2.5 broadcast_in_dim.68
  672.2 6.4 scatter_fusion
  678.6 7.4 all-to-all-start
  686.0 186.7 %psum.7 = f32[]{:T(128)} all-reduce(f32[]{:T(128)} %get-tuple-element.72), channel_id=1, replica_groups=mesh['ctx'=64,'tp'=8] {'ctx','tp'}, use_global_device_ids=true, to_apply=%region_10.12 | all-reduce | flops 1 | bytes 8 | tf_op jit(solution)/shard_map/psum | solution.py:96
  874.6 2.4 reduce_sum.36
  (181 shorter events, 45.7 us)
Async XLA Ops:
  7.2 6.5 copy-start
  7.2 9.2 %copy-start.8 = (bf16[256,1024]{1,0:T(8,128)(2,1)S(1)}, bf16[256,1024]{1,0:T(8,128)(2,1)}, u32[]{:S(2)}) copy-start(bf16[256,1024]{1,0:T(8,128)(2,1)} %param.12) | copy-start | bytes 1572868
  7.2 263.5 %all-gather.5.cloned.1.call-start = ((), (), s32[]{:S(2)}) async-start(), calls=%async_computation.2 | async-start | bytes 1064960 | tf_op jit(solution)/shard_map/all_gather | solution.py:21
  7.9 562.4 %all-gather.3.cloned.1.call-start = ((), (), s32[]{:S(2)}) async-start(), calls=%async_computation.1 | async-start | bytes 1064960 | tf_op jit(solution)/shard_map/all_gather | solution.py:20
  572.4 1.4 copy-start.6
  577.8 1.5 copy-start.1
  579.3 2.5 copy-start.4
  580.7 2.4 copy-start.2
  580.7 3.4 copy-start.7
  584.0 1.4 copy-start.6
  589.4 1.5 copy-start.1
  590.9 2.5 copy-start.4
  592.3 2.4 copy-start.2
  592.3 3.4 copy-start.7
  595.7 1.4 copy-start.6
  601.0 1.5 copy-start.1
  602.5 2.5 copy-start.4
  603.9 2.4 copy-start.2
  603.9 3.4 copy-start.7
  606.3 1.0 copy-start.5
  607.3 1.4 copy-start.6
  612.6 1.5 copy-start.1
  614.1 2.5 copy-start.4
  615.5 2.4 copy-start.2
  615.5 3.4 copy-start.7
  618.9 1.4 copy-start.6
  624.3 1.5 copy-start.1
  625.7 2.5 copy-start.4
  627.1 2.4 copy-start.2
  627.1 3.4 copy-start.7
  630.5 1.4 copy-start.6
  635.9 1.5 copy-start.1
  637.3 2.5 copy-start.4
  638.7 2.4 copy-start.2
  638.7 3.4 copy-start.7
  642.1 1.4 copy-start.6
  647.5 1.5 copy-start.1
  649.0 2.5 copy-start.4
  650.3 2.4 copy-start.2
  650.4 3.4 copy-start.7
  653.7 1.4 copy-start.6
  659.1 1.5 copy-start.1
  660.6 2.5 copy-start.4
  662.0 2.4 copy-start.2
  662.0 3.4 copy-start.7
  665.3 1.6 copy-start.3
  678.6 194.1 %copy-start.9 = (bf16[8,256,1,128]{3,1,2,0:T(8,128)(2,1)S(1)}, bf16[8,256,1,128]{3,1,2,0:T(8,128)(2,1)}, u32[]{:S(2)}) copy-start(bf16[8,256,1,128]{3,1,2,0:T(8,128)(2,1)} %get-tuple-element.69) | copy-start | bytes 1572868
  678.6 196.0 %all-to-all-start = ((f32[64,64,256]{2,1,0:T(8,128)}), f32[64,64,256]{2,1,0:T(8,128)}, u32[]{:S(2)}, u32[]{:S(2)}) async-start(f32[64,64,256]{2,1,0:T(8,128)} %scatter_fusion), calls=%async_computation | async-start | bytes 8388608 | tf_op jit(solution)/shard_map/all_to_all | solution.py:92
  (7 other events, 6.9 us)
Sparse Core Ops, SparseCore 0:
  10.1 260.5 all-gather.4
  272.8 297.4 all-gather.2
where the time goes:
time: 887 us; the launch traced here: 886 us
  waiting for transfers between devices  552 us (62%)
  blocking collectives  187 us (21%)
  matrix products  61.8 us (7%)
  local copies, waits for them, and re-layouts  30.3 us (3%)
  other arithmetic  24.2 us (3%)
  between operations  16.7 us (2%)
    all_gather x1, waiting for transfers between devices, per_device(): lax.all_gather(image_keys, 'ctx', axis=0, tiled=True)  298 us
    all_gather x1, waiting for transfers between devices, per_device(): lax.all_gather(image_values, 'ctx', axis=0, tiled=True)  253 us
    psum x1, blocking collectives, per_device(): gate_total = lax.psum(gate_acc, ('ctx', 'tp'))  187 us
  transfers between devices with their start and end apart: 3, of which 2 were waited for; matrix products, arithmetic and copies ran while one was open for 1% of the time, Pallas kernels for 0%

commit v1 on v0

--- a/solution.py
+++ b/solution.py
@@ -6,6 +6,11 @@
 
 HD = 128
 BLK = 128
+
+
+def by_each_axis(value, axis_one, axis_two):
+    inner = lax.psum(value, axis_one)
+    return lax.psum(inner, axis_two)
 
 
 def per_device(queries, cotangent, image_keys, image_values, attn_gate, block_mask, image_owner):
@@ -93,7 +98,7 @@
     summed = jnp.sum(received, axis=0, keepdims=True)
     key_grad = summed[:, :, : local_kv * HD].astype(jnp.bfloat16)
     value_grad = summed[:, :, local_kv * HD :].astype(jnp.bfloat16)
-    gate_total = lax.psum(gate_acc, ("ctx", "tp"))
+    gate_total = by_each_axis(gate_acc, "ctx", "tp")
     term_count = tok_dev * lax.axis_size("ctx") * local_heads * lax.axis_size("tp") * HD
     gate_grad = ((1.0 - gate_value * gate_value) * gate_total / math.sqrt(term_count)).reshape(1)
     return (query_grad, key_grad, value_grad, gate_grad)

time: 887 us -> 955 us (1.077)
  blocking collectives: 187 us -> 255 us
    psum x1 -> x2, blocking collectives: 187 us -> 255 us  [the longest x1 202 us: by_each_axis(): inner = lax.psum(value, axis_one)]
where the time goes in v1:
time: 955 us; the launch traced here: 954 us
  waiting for transfers between devices  552 us (58%)
  blocking collectives  255 us (27%)
  matrix products  61.8 us (6%)
  local copies, waits for them, and re-layouts  30.3 us (3%)
  other arithmetic  24.2 us (3%)
  between operations  16.7 us (2%)
    all_gather x1, waiting for transfers between devices, per_device(): lax.all_gather(image_keys, 'ctx', axis=0, tiled=True)  298 us
    all_gather x1, waiting for transfers between devices, per_device(): lax.all_gather(image_values, 'ctx', axis=0, tiled=True)  253 us
    psum x1, blocking collectives, by_each_axis(): inner = lax.psum(value, axis_one)  202 us
    psum x1, blocking collectives, by_each_axis(): return lax.psum(inner, axis_two)  52.2 us
  transfers between devices with their start and end apart: 3, of which 2 were waited for; matrix products, arithmetic and copies ran while one was open for 1% of the time, Pallas kernels for 0%

profile of v1, /device:TPU:1, one launch (start us, length us, event | category | flops | bytes accessed | tf_op | source)
XLA Modules:
  0.0 953.7 jit_solution(13649404426227503398)
XLA Ops:
  10.9 2.0 top_k.11
  15.1 1.2 copy.35
  17.4 253.3 %all-gather.5.cloned.1.call-done = bf16[64,64,128]{2,1,0:T(8,128)(2,1)} async-done(((bf16[1,64,128]{2,1,0:T(8,128)(2,1)}), bf16[64,64,128]{2,1,0:T(8,128)(2,1)}) %all-gather.5.cloned.1.call-update) | async-done | bytes 1048592 | tf_op jit(solution)/shard_map/all_gather | solution.py:26
  270.7 1.9 gather_fusion.4
  272.6 297.7 %all-gather.3.cloned.1.call-done = bf16[64,64,128]{2,1,0:T(8,128)(2,1)} async-done(((bf16[1,64,128]{2,1,0:T(8,128)(2,1)}), bf16[64,64,128]{2,1,0:T(8,128)(2,1)}) %all-gather.3.cloned.1.call-update) | async-done | bytes 1048592 | tf_op jit(solution)/shard_map/all_gather | solution.py:25
  570.4 1.9 gather_fusion.3
  572.4 92.9 %while.17 = (s32[]{:T(128)}, f32[2048,1,128]{0,2,1:T(8,128)}, f32[2048,1,128]{0,2,1:T(8,128)}, f32[]{:T(128)}, bf16[8,256,1,128]{3,1,2,0:T(8,128)(2,1)}, /*index...) while((s32[]{:T(128)}, f32[2048,1,128]{0,2,1:T(8,128)}, ...), condition=%wide.region_7.9_spmd.clone, body=%wide.region_2.8_spmd.clone.sunk | while | flops 814710016 | bytes 48644448 | solution.py:82
  575.2 1.9 fusion.68
  577.8 1.4 fusion.69
  579.3 1.4 fusion.71
  581.8 1.3 fusion.70
  586.8 1.9 fusion.68
  589.4 1.4 fusion.69
  590.9 1.4 fusion.71
  593.4 1.3 fusion.70
  598.4 1.9 fusion.68
  601.0 1.4 fusion.69
  602.5 1.4 fusion.71
  605.0 1.3 fusion.70
  610.1 1.9 fusion.68
  612.7 1.4 fusion.69
  614.1 1.4 fusion.71
  616.6 1.3 fusion.70
  621.7 1.9 fusion.68
  624.3 1.4 fusion.69
  625.7 1.4 fusion.71
  628.2 1.3 fusion.70
  633.3 1.9 fusion.68
  635.9 1.4 fusion.69
  637.3 1.4 fusion.71
  639.8 1.3 fusion.70
  644.9 1.9 fusion.68
  647.5 1.4 fusion.69
  649.0 1.4 fusion.71
  651.4 1.3 fusion.70
  656.5 1.9 fusion.68
  659.1 1.4 fusion.69
  660.6 1.4 fusion.71
  663.1 1.3 fusion.70
  665.3 1.6 copy.40
  667.0 1.3 copy.41
  668.3 1.4 maximum_select_fusion
  669.8 2.5 broadcast_in_dim.68
  672.2 6.4 scatter_fusion
  678.6 7.4 all-to-all-start
  686.0 202.5 %psum.14 = f32[]{:T(128)} all-reduce(f32[]{:T(128)} %get-tuple-element.72), channel_id=1, replica_groups=mesh['ctx'=64,'tp'=8] {'ctx'}, use_global_device_ids=true, to_apply=%region_10.12 | all-reduce | flops 1 | bytes 8 | tf_op jit(solution)/shard_map/psum | solution.py:12
  888.5 52.2 %psum.15 = f32[]{:T(128)} all-reduce(f32[]{:T(128)} %psum.14), channel_id=1, replica_groups=mesh['ctx'=64,'tp'=8] {'tp'}, use_global_device_ids=true, to_apply=%region_11.13 | all-reduce | flops 1 | bytes 8 | tf_op jit(solution)/shard_map/psum | solution.py:13
  942.6 2.4 reduce_sum.36
  (182 shorter events, 46.8 us)
Async XLA Ops:
  7.2 6.5 copy-start
  7.2 9.2 copy-start.8
  7.2 263.5 %all-gather.5.cloned.1.call-start = ((), (), s32[]{:S(2)}) async-start(), calls=%async_computation.2 | async-start | bytes 1064960 | tf_op jit(solution)/shard_map/all_gather | solution.py:26
  7.9 562.4 %all-gather.3.cloned.1.call-start = ((), (), s32[]{:S(2)}) async-start(), calls=%async_computation.1 | async-start | bytes 1064960 | tf_op jit(solution)/shard_map/all_gather | solution.py:25
  572.4 1.4 copy-start.6
  577.8 1.5 copy-start.1
  579.3 2.5 copy-start.4
  580.7 2.4 copy-start.2
  580.7 3.4 copy-start.7
  584.0 1.4 copy-start.6
  589.4 1.5 copy-start.1
  590.9 2.5 copy-start.4
  592.3 2.4 copy-start.2
  592.3 3.4 copy-start.7
  595.7 1.4 copy-start.6
  601.0 1.5 copy-start.1
  602.5 2.5 copy-start.4
  603.9 2.4 copy-start.2
  603.9 3.4 copy-start.7
  606.3 1.0 copy-start.5
  607.3 1.4 copy-start.6
  612.6 1.5 copy-start.1
  614.1 2.5 copy-start.4
  615.5 2.4 copy-start.2
  615.5 3.4 copy-start.7
  618.9 1.4 copy-start.6
  624.3 1.5 copy-start.1
  625.7 2.5 copy-start.4
  627.1 2.4 copy-start.2
  627.1 3.4 copy-start.7
  630.5 1.4 copy-start.6
  635.9 1.5 copy-start.1
  637.3 2.5 copy-start.4
  638.7 2.4 copy-start.2
  638.7 3.4 copy-start.7
  642.1 1.4 copy-start.6
  647.5 1.5 copy-start.1
  649.0 2.5 copy-start.4
  650.3 2.4 copy-start.2
  650.4 3.4 copy-start.7
  653.7 1.4 copy-start.6
  659.1 1.5 copy-start.1
  660.6 2.5 copy-start.4
  662.0 2.4 copy-start.2
  662.0 3.4 copy-start.7
  665.3 1.6 copy-start.3
  678.6 262.1 %copy-start.9 = (bf16[8,256,1,128]{3,1,2,0:T(8,128)(2,1)S(1)}, bf16[8,256,1,128]{3,1,2,0:T(8,128)(2,1)}, u32[]{:S(2)}) copy-start(bf16[8,256,1,128]{3,1,2,0:T(8,128)(2,1)} %get-tuple-element.69) | copy-start | bytes 1572868
  678.6 264.0 %all-to-all-start = ((f32[64,64,256]{2,1,0:T(8,128)}), f32[64,64,256]{2,1,0:T(8,128)}, u32[]{:S(2)}, u32[]{:S(2)}) async-start(f32[64,64,256]{2,1,0:T(8,128)} %scatter_fusion), calls=%async_computation | async-start | bytes 8388608 | tf_op jit(solution)/shard_map/all_to_all | solution.py:97
  (7 other events, 6.9 us)
Sparse Core Ops, SparseCore 0:
  10.1 260.5 all-gather.4
  272.8 297.4 all-gather.2
